TPU v7x, 32 devices: a whole 2x2x4 slice. The times are simulated.
32 devices in a mesh: ctx: 8 (over z, y), chan: 4 (over x, core).
Axes of the slice: x: 2, y: 2, z: 4, core: 2. Of those that a mesh axis runs over, the one named last changes fastest.
Arguments:
- query_in: bfloat16 [1024, 8192], P(('ctx', 'chan')), may hold values from -6 to 6
- key_in: bfloat16 [1024, 8192], P(('ctx', 'chan')), may hold values from -6 to 6
- value_in: bfloat16 [1024, 8192], P(('ctx', 'chan')), may hold values from -6 to 6
- cotangent: bfloat16 [1024, 8192], P(('ctx', 'chan')), may hold values from -6 to 6
- residues: float32 [16, 8192], P(None, 'chan'), may hold values from -1.5 to 1.5
- decay_rate: float32 [16, 8192], P(None, 'chan'), may hold values from 1e-05 to 0.1
- short_weight: float32 [3, 3, 8192], P(None, None, 'chan'), may hold values from -3 to 3
- doc_lengths: int32 [8], replicated, may hold values from 1 to 512, 1024 in all
Outputs:
- output: bfloat16 [1024, 8192], P(('ctx', 'chan'))
- d_query_in: bfloat16 [1024, 8192], P(('ctx', 'chan'))
- d_key_in: bfloat16 [1024, 8192], P(('ctx', 'chan'))
- d_value_in: bfloat16 [1024, 8192], P(('ctx', 'chan'))
- d_resid: float32 [16, 8192], P(None, 'chan')
- d_short: float32 [3, 3, 8192], P(None, None, 'chan')
Inputs may be any that keep to these rules, and one draw needn't show every extreme that they name: `doc_lengths`: the lengths of the 8 documents sum to 1024, and the longest has exactly 512 tokens.
All inputs are finite; a program needn't handle non-finite values.
Results may differ from a plain program's by a relative error of at most 0.001.
Values may be sent and summed in bfloat16 or wider, within the bound.
A program may use at most 128 MiB of HBM per device.

v0:
```python
import functools

import jax
import jax.numpy as jnp
from jax import lax
from jax.experimental import pallas as pl
from jax.experimental.pallas import tpu as pltpu
from jax.sharding import PartitionSpec as P

MESH = pl.DeviceIdType.MESH
sub, lanes = 8, 128
wide = sub * lanes
step_rows = 4


def total_of(terms):
    terms = list(terms)
    while len(terms) > 1:
        paired = [a + b for a, b in zip(terms[::2], terms[1::2])]
        terms = paired + ([terms[-1]] if len(terms) % 2 else [])
    return terms[0]


def mixer(
    shape,
    flags, gates, reach, query_in, key_in, value_in, cotangent, table, mixing, kappa, taps,
    output, d_query, d_key, d_value, d_resid, d_short,
    inbox, stage, rows, grads, feats, product, grad_pre, d_feat, outbox,
    state_send, state_recv, part, shares, summed, whole,
    in_send, in_recv, local_sem, tail_send, tail_recv, far_send, far_recv,
    head_send, head_recv, out_send, out_recv, share_send, share_recv, whole_send, whole_recv,
):
    n, width, span, count, modes, tap_count, piece, chunks = shape
    own_rows = count // width
    pitch = stage.shape[1] // sub
    rim = tap_count - 1
    ctx = lax.axis_index("ctx")
    chan = lax.axis_index("chan")
    sources = (query_in, key_in, value_in, cotangent)
    targets = (output, d_query, d_key, d_value)

    def peer_chan(k):
        return lax.rem(chan + k, width)

    def at_chan(c):
        return (ctx, c)

    def at_ctx(c):
        return (c, chan)

    barrier = pltpu.get_barrier_semaphore()
    for k in range(1, width):
        pl.semaphore_signal(barrier, inc=1, device_id=at_chan(peer_chan(k)), device_id_type=MESH)

    def greet(k, carry):
        pl.semaphore_signal(barrier, inc=1, device_id=at_ctx(lax.rem(ctx + k, n)), device_id_type=MESH)
        return carry

    lax.fori_loop(1, n, greet, 0)
    pl.semaphore_wait(barrier, width - 1 + n - 1)

    def columns(owner, q):
        return pl.ds(pl.multiple_of((owner * chunks + q) * wide, wide), wide)

    def in_copy(q, a, k):
        peer = peer_chan(k)
        return pltpu.make_async_remote_copy(
            src_ref=sources[a].at[:, columns(peer, q)],
            dst_ref=inbox.at[a, q, chan],
            send_sem=in_send.at[q, a, k],
            recv_sem=in_recv.at[q, a, k],
            device_id=at_chan(peer),
            device_id_type=MESH,
        )

    def in_arrival(q, a, k):
        return pltpu.make_async_remote_copy(
            src_ref=sources[a].at[:, columns(chan, q)],
            dst_ref=inbox.at[a, q, lax.rem(chan + width - k, width)],
            send_sem=in_send.at[q, a, k],
            recv_sem=in_recv.at[q, a, k],
            device_id=at_chan(peer_chan(k)),
            device_id_type=MESH,
        )

    def in_local(q, a):
        return pltpu.make_async_copy(
            sources[a].at[:, columns(chan, q)], inbox.at[a, q, chan], local_sem.at[0, q, a]
        )

    for q in range(chunks):
        for a in range(4):
            for k in range(1, width):
                in_copy(q, a, k).start()
            in_local(q, a).start()

    def tail_copy(q, i):
        return pltpu.make_async_remote_copy(
            src_ref=rows.at[q, i, pl.ds(count, rim)],
            dst_ref=rows.at[q, i, pl.ds(0, rim)],
            send_sem=tail_send.at[q, i],
            recv_sem=tail_recv.at[q, i],
            device_id=at_ctx(lax.rem(ctx + 1, n)),
            device_id_type=MESH,
        )

    def head_copy(q, i):
        return pltpu.make_async_remote_copy(
            src_ref=d_feat.at[q, i, pl.ds(0, rim)],
            dst_ref=d_feat.at[q, i, pl.ds(count, rim)],
            send_sem=head_send.at[q, i],
            recv_sem=head_recv.at[q, i],
            device_id=at_ctx(lax.rem(ctx + n - 1, n)),
            device_id_type=MESH,
        )

    def far_copy(q, way, d):
        partner = lax.rem(ctx + d, n) if way == 0 else lax.rem(ctx + n - d, n)
        return pltpu.make_async_remote_copy(
            src_ref=state_send.at[q, way],
            dst_ref=state_recv.at[q, way, d - 1],
            send_sem=far_send.at[q, way, d - 1],
            recv_sem=far_recv.at[q, way, d - 1],
            device_id=at_ctx(partner),
            device_id_type=MESH,
        )

    def sends_far(way, d):
        return ctx + d < n if way == 0 else ctx >= d

    def gets_far(way, d):
        return ctx >= d if way == 0 else ctx + d < n

    def far_start(q, way):
        for d in range(1, span + 1):
            @pl.when(sends_far(way, d))
            def _():
                far_copy(q, way, d).start()

    def far_wait(q, way):
        for d in range(1, span + 1):
            @pl.when(gets_far(way, d))
            def _():
                far_copy(q, way, d).wait_recv()

            @pl.when(jnp.logical_not(gets_far(way, d)))
            def _():
                state_recv[q, way, d - 1] = jnp.zeros((modes, sub, lanes), jnp.float32)

    def mode_block(q):
        return pl.ds(q * sub, sub)

    def first_pass(q):
        for a in range(4):
            for k in range(1, width):
                in_arrival(q, a, k).wait_recv()
            in_local(q, a).wait()

        for a in range(4):
            def place(s, carry):
                for j in range(sub):
                    tile = inbox[a, q, s, :, pl.ds(j * lanes, lanes)].astype(jnp.float32)
                    stage[a, pl.ds(pl.multiple_of(j * pitch + s * own_rows, 8), own_rows), :] = tile
                return carry

            lax.fori_loop(0, width, place, 0)

        def lift(b, carry):
            for u in range(step_rows):
                t = b * step_rows + u
                for a in range(3):
                    rows[q, a, t + rim] = stage[a, pl.ds(t, sub, stride=pitch), :]
                grads[q, t] = stage[3, pl.ds(t, sub, stride=pitch), :]
            return carry

        lax.fori_loop(0, count // step_rows, lift, 0)
        for i in range(3):
            tail_copy(q, i).start()
        for i in range(3):
            tail_copy(q, i).wait_recv()

        decay = [table[0, m, mode_block(q), :] for m in range(modes)]
        tap = [[taps[i * tap_count + j, mode_block(q), :] for j in range(tap_count)] for i in range(3)]

        def featurize(b, states):
            for u in range(step_rows):
                t = b * step_rows + u
                made = []
                for i in range(3):
                    made.append(
                        tap[i][0] * rows[q, i, t + rim]
                        + total_of(
                            [
                                (gates[j, t] * tap[i][j]) * rows[q, i, t + rim - j]
                                for j in range(1, tap_count)
                            ]
                        )
                    )
                value = made[1] * made[2]
                for i in range(3):
                    feats[q, i, t] = made[i]
                product[q, t] = value
                grad_pre[q, t] = grads[q, t] * made[0]
                masked = gates[tap_count, t] * value
                states = tuple(decay[m] * states[m] + masked for m in range(modes))
            return states

        zeros = tuple(jnp.zeros((sub, lanes), jnp.float32) for _ in range(modes))
        ends = lax.fori_loop(0, count // step_rows, featurize, zeros)
        for m in range(modes):
            state_send[q, 0, m] = ends[m]
        far_start(q, 0)

        def back(b, states):
            for u in range(step_rows):
                t = count - 1 - b * step_rows - u
                masked = gates[0, t] * grad_pre[q, t]
                states = tuple(decay[m] * states[m] + masked for m in range(modes))
            return states

        ends = lax.fori_loop(0, count // step_rows, back, zeros)
        for m in range(modes):
            state_send[q, 1, m] = ends[m]
        far_start(q, 1)

    def entering(q, way):
        far_wait(q, way)
        carried = []
        for m in range(modes):
            power = table[0, m, mode_block(q), :]
            for _ in range(count.bit_length() - 1):
                power = power * power

            def nearer(s, value, m=m, power=power):
                d = span - s
                return power * value + reach[way, d - 1] * state_recv[q, way, d - 1, m]

            carried.append(lax.fori_loop(0, span, nearer, jnp.zeros((sub, lanes), jnp.float32)))
        return tuple(carried)

    def short_terms(q, i, t, grad):
        return [grad * rows[q, i, t + rim]] + [
            (gates[j, t] * grad) * rows[q, i, t + rim - j] for j in range(1, tap_count)
        ]

    def share_copy(q, k):
        peer = lax.rem(ctx + k, n)
        return pltpu.make_async_remote_copy(
            src_ref=part.at[q, peer],
            dst_ref=shares.at[q, k],
            send_sem=share_send.at[q, k],
            recv_sem=share_recv.at[q, k],
            device_id=at_ctx(peer),
            device_id_type=MESH,
        )

    def whole_copy(q, k):
        return pltpu.make_async_remote_copy(
            src_ref=summed.at[q],
            dst_ref=whole.at[q, ctx],
            send_sem=whole_send.at[q, k],
            recv_sem=whole_recv.at[q, k],
            device_id=at_ctx(lax.rem(ctx + k, n)),
            device_id_type=MESH,
        )

    def whole_arrival(q, k):
        return pltpu.make_async_remote_copy(
            src_ref=summed.at[q],
            dst_ref=whole.at[q, lax.rem(ctx + n - k, n)],
            send_sem=whole_send.at[q, k],
            recv_sem=whole_recv.at[q, k],
            device_id=at_ctx(lax.rem(ctx + k, n)),
            device_id_type=MESH,
        )

    def out_copy(q, a, k):
        peer = peer_chan(k)
        return pltpu.make_async_remote_copy(
            src_ref=outbox.at[a, q, peer],
            dst_ref=targets[a].at[:, columns(chan, q)],
            send_sem=out_send.at[q, a, k],
            recv_sem=out_recv.at[q, a, k],
            device_id=at_chan(peer),
            device_id_type=MESH,
        )

    def out_arrival(q, a, k):
        origin = lax.rem(chan + width - k, width)
        return pltpu.make_async_remote_copy(
            src_ref=outbox.at[a, q, origin],
            dst_ref=targets[a].at[:, columns(origin, q)],
            send_sem=out_send.at[q, a, k],
            recv_sem=out_recv.at[q, a, k],
            device_id=at_chan(peer_chan(k)),
            device_id_type=MESH,
        )

    def out_local(q, a):
        return pltpu.make_async_copy(
            outbox.at[a, q, chan], targets[a].at[:, columns(chan, q)], local_sem.at[1, q, a]
        )

    def send_out(q, a):
        def pack(s, carry):
            for j in range(sub):
                tile = stage[a, pl.ds(pl.multiple_of(j * pitch + s * own_rows, 8), own_rows), :]
                outbox[a, q, s, :, pl.ds(j * lanes, lanes)] = tile.astype(jnp.bfloat16)
            return carry

        lax.fori_loop(0, width, pack, 0)
        for k in range(1, width):
            out_copy(q, a, k).start()
        out_local(q, a).start()

    def put_part(q, index, value):
        part[q, index // piece, index % piece] = value

    def second_pass(q):
        mix = [mixing[m, mode_block(q), :] for m in range(modes)]
        tap = [[taps[i * tap_count + j, mode_block(q), :] for j in range(tap_count)] for i in range(3)]
        zero = jnp.zeros((sub, lanes), jnp.float32)
        carried = entering(q, 1)

        def reverse(b, carry):
            states, sums = carry
            for u in range(step_rows):
                t = count - 1 - b * step_rows - u
                flag = flags[t + 1]
                grad_row = grad_pre[q, t]
                states = tuple(
                    table[flag, m, mode_block(q), :] * states[m] + grad_row for m in range(modes)
                )
                mixed = total_of([mix[m] * states[m] for m in range(modes)])
                pair = (mixed * feats[q, 2, t], mixed * feats[q, 1, t])
                d_feat[q, 1, t] = pair[0]
                d_feat[q, 2, t] = pair[1]
                terms = short_terms(q, 1, t, pair[0]) + short_terms(q, 2, t, pair[1])
                sums = tuple(s + x for s, x in zip(sums, terms))
            return states, sums

        _, sums = lax.fori_loop(
            0, count // step_rows, reverse, (carried, (zero,) * (2 * tap_count))
        )
        head_copy(q, 1).start()
        head_copy(q, 2).start()
        for x in range(2 * tap_count):
            put_part(q, modes + tap_count + x, sums[x])
        carried = entering(q, 0)

        def advance(b, carry):
            states, found, sums = carry
            for u in range(step_rows):
                t = b * step_rows + u
                flag = flags[t]
                value = product[q, t]
                grad_row = grad_pre[q, t]
                states = tuple(
                    table[flag, m, mode_block(q), :] * states[m] + value for m in range(modes)
                )
                mixed = total_of([mix[m] * states[m] for m in range(modes)])
                found = tuple(found[m] + grad_row * states[m] for m in range(modes))
                stage[0, pl.ds(t, sub, stride=pitch), :] = feats[q, 0, t] * mixed
                grad = grads[q, t] * mixed
                d_feat[q, 0, t] = grad
                sums = tuple(s + x for s, x in zip(sums, short_terms(q, 0, t, grad)))
            return states, found, sums

        start = (carried, (zero,) * modes, (zero,) * tap_count)
        _, found, sums = lax.fori_loop(0, count // step_rows, advance, start)
        head_copy(q, 0).start()
        send_out(q, 0)
        for m in range(modes):
            put_part(q, m, kappa[m, mode_block(q), :] * found[m])
        for x in range(tap_count):
            put_part(q, modes + x, sums[x])
        for x in range(modes + 3 * tap_count, n * piece):
            put_part(q, x, zero)

        def spread(k, carry):
            share_copy(q, k).start()
            return carry

        lax.fori_loop(1, n, spread, 0)
        for i in (1, 2, 0):
            head_copy(q, i).wait_recv()

            def undo(b, carry):
                for u in range(step_rows):
                    t = b * step_rows + u
                    stage[1 + i, pl.ds(t, sub, stride=pitch), :] = tap[i][0] * d_feat[q, i, t] + total_of(
                        [
                            (gates[j, t + j] * tap[i][j]) * d_feat[q, i, t + j]
                            for j in range(1, tap_count)
                        ]
                    )
                return carry

            lax.fori_loop(0, count // step_rows, undo, 0)
            send_out(q, 1 + i)

    def gather(q):
        def take(k, carry):
            share_copy(q, k).wait_recv()
            return carry

        lax.fori_loop(1, n, take, 0)
        shares[q, 0] = part[q, ctx]

        def add(k, value):
            return value + shares[q, k]

        total = lax.fori_loop(1, n, add, shares[q, 0])
        summed[q] = total
        whole[q, ctx] = total

        def spread(k, carry):
            whole_copy(q, k).start()
            return carry

        lax.fori_loop(1, n, spread, 0)

    def write(q):
        def take(k, carry):
            whole_arrival(q, k).wait_recv()
            return carry

        lax.fori_loop(1, n, take, 0)
        for x in range(modes):
            value = whole[q, x // piece, x % piece]
            for j in range(sub):
                d_resid[pl.ds(x, 1), pl.ds((q * sub + j) * lanes, lanes)] = value[j : j + 1]
        for y in range(3 * tap_count):
            x = modes + y
            value = whole[q, x // piece, x % piece]
            for j in range(sub):
                d_short[pl.ds(y, 1), pl.ds((q * sub + j) * lanes, lanes)] = value[j : j + 1]

    for q in range(chunks):
        first_pass(q)
    for q in range(chunks):
        second_pass(q)
        if q:
            gather(q - 1)
    gather(chunks - 1)
    for q in range(chunks):
        write(q)

    for q in range(chunks):
        for a in range(4):
            for k in range(1, width):
                in_copy(q, a, k).wait_send()
                out_copy(q, a, k).wait_send()
                out_arrival(q, a, k).wait_recv()
            out_local(q, a).wait()
        for i in range(3):
            tail_copy(q, i).wait_send()
            head_copy(q, i).wait_send()
        for way in range(2):
            for d in range(1, span + 1):
                @pl.when(sends_far(way, d))
                def _():
                    far_copy(q, way, d).wait_send()

        def drain(k, carry):
            share_copy(q, k).wait_send()
            whole_copy(q, k).wait_send()
            return carry

        lax.fori_loop(1, n, drain, 0)


def shards(n, width, query_in, key_in, value_in, cotangent, residues, decay_rate, short_weight, doc_lengths):
    own_rows, channels = query_in.shape
    modes, local = residues.shape
    tap_count = short_weight.shape[1]
    rim = tap_count - 1
    count = own_rows * width
    chunks = local // wide
    tiles = local // lanes
    span = max(n // 2, 1)
    first_row = lax.axis_index("ctx") * count
    order = jnp.arange(doc_lengths.shape[0], dtype=jnp.int32)
    starts = jnp.sum(jnp.where(order[None, :] < order[:, None], doc_lengths[None, :], 0), axis=1)
    positions = first_row - rim + jnp.arange(count + 2 * rim, dtype=jnp.int32)
    hits = jnp.any(positions[:, None] == starts[None, :], axis=1)
    after = positions[rim:]
    gate_rows = []
    behind = (after < n * count) & (after >= 0)
    gate_rows_tail = []
    keep = behind
    for j in range(1, tap_count):
        keep = keep & ~hits[rim - j + 1 : rim - j + 1 + count + rim]
        gate_rows_tail.append(keep & (after >= j))
    inside = (starts[None, :] >= first_row) & (starts[None, :] <= after[:, None])
    gate_rows.append(~jnp.any(inside, axis=1))
    gate_rows += gate_rows_tail
    later = (starts[None, :] > after[:, None]) & (starts[None, :] < first_row + count)
    gate_rows.append(~jnp.any(later, axis=1))
    gates = jnp.stack(gate_rows).astype(jnp.float32)
    flags = hits[rim:].astype(jnp.int32)
    hop = jnp.arange(1, span + 1, dtype=jnp.int32)[:, None]
    early = (starts[None, :] >= first_row - (hop - 1) * count) & (starts[None, :] < first_row)
    late = (starts[None, :] >= first_row + count) & (starts[None, :] < first_row + hop * count)
    reach = jnp.stack([~jnp.any(early, axis=1), ~jnp.any(late, axis=1)]).astype(jnp.float32)

    decays = jnp.exp(-decay_rate)
    kappa = jnp.sqrt(1.0 - jnp.exp(-2.0 * decay_rate))
    mixing = residues * kappa
    table = jnp.stack([decays, jnp.zeros_like(decays)]).reshape(2, modes, tiles, lanes)
    mixing = mixing.reshape(modes, tiles, lanes)
    kappa = kappa.reshape(modes, tiles, lanes)
    taps = short_weight.reshape(3 * tap_count, tiles, lanes)

    pieces = modes + 3 * tap_count
    piece = -(-pieces // n)
    pitch = count + 8
    f32, bf16 = jnp.float32, jnp.bfloat16
    dma = pltpu.SemaphoreType.DMA
    anywhere = pl.BlockSpec(memory_space=pl.ANY)
    vmem = pl.BlockSpec(memory_space=pltpu.VMEM)
    smem = pl.BlockSpec(memory_space=pltpu.SMEM)
    shape = (n, width, span, count, modes, tap_count, piece, chunks)
    token = (sub, lanes)
    results = pl.pallas_call(
        functools.partial(mixer, shape),
        out_shape=[jax.ShapeDtypeStruct((own_rows, channels), bf16)] * 4
        + [
            jax.ShapeDtypeStruct((modes, local), f32),
            jax.ShapeDtypeStruct((3 * tap_count, local), f32),
        ],
        in_specs=[smem] * 3 + [anywhere] * 4 + [vmem] * 4,
        out_specs=[anywhere] * 4 + [vmem] * 2,
        scratch_shapes=[
            pltpu.VMEM((4, chunks, width, own_rows, wide), bf16),
            pltpu.VMEM((4, sub * pitch, lanes), f32),
            pltpu.VMEM((chunks, 3, count + rim) + token, f32),
            pltpu.VMEM((chunks, count) + token, f32),
            pltpu.VMEM((chunks, 3, count) + token, f32),
            pltpu.VMEM((chunks, count) + token, f32),
            pltpu.VMEM((chunks, count) + token, f32),
            pltpu.VMEM((chunks, 3, count + rim) + token, f32),
            pltpu.VMEM((4, chunks, width, own_rows, wide), bf16),
            pltpu.VMEM((chunks, 2, modes) + token, f32),
            pltpu.VMEM((chunks, 2, span, modes) + token, f32),
            pltpu.VMEM((chunks, n, piece) + token, f32),
            pltpu.VMEM((chunks, n, piece) + token, f32),
            pltpu.VMEM((chunks, piece) + token, f32),
            pltpu.VMEM((chunks, n, piece) + token, f32),
            dma((chunks, 4, width)),
            dma((chunks, 4, width)),
            dma((2, chunks, 4)),
            dma((chunks, 3)),
            dma((chunks, 3)),
            dma((chunks, 2, span)),
            dma((chunks, 2, span)),
            dma((chunks, 3)),
            dma((chunks, 3)),
            dma((chunks, 4, width)),
            dma((chunks, 4, width)),
            dma((chunks, n)),
            dma((chunks, n)),
            dma((chunks, n)),
            dma((chunks, n)),
        ],
        compiler_params=pltpu.CompilerParams(
            collective_id=0, has_side_effects=True, vmem_limit_bytes=48 * 1024 * 1024
        ),
    )(flags, gates, reach, query_in, key_in, value_in, cotangent, table, mixing, kappa, taps)
    return (*results[:5], results[5].reshape(short_weight.shape))


def solution(mesh):
    tokens = P(("ctx", "chan"), None)
    return jax.shard_map(
        functools.partial(shards, mesh.shape["ctx"], mesh.shape["chan"]),
        mesh=mesh,
        in_specs=(tokens,) * 4 + (P(None, "chan"), P(None, "chan"), P(None, None, "chan"), P()),
        out_specs=(tokens,) * 4 + (P(None, "chan"), P(None, None, "chan")),
        check_vma=False,
    )
```

profile of v0, /device:TPU:13, one launch (start us, length us, event | category | flops | bytes accessed | tf_op | source)
XLA Modules:
  0.0 81.2 jit_solution(15636671521411171889)
XLA Ops:
  0.6 0.0 copy-start.6
  0.6 0.0 copy-start.5
  0.7 0.0 copy-start.4
  0.7 0.6 copy-done.6
  1.3 0.1 select_reduce_fusion
  1.4 0.1 compare_reduce_fusion
  1.5 0.1 slice.11
  1.6 0.1 compare_and_fusion.1
  1.6 0.1 compare_and_fusion
  1.8 0.2 and_reduce_fusion.3
  2.0 0.1 and_reduce_fusion.1
  2.2 0.9 %reshape.102.taps = f32[9,16,128]{2,1,0:T(8,128)S(1)} reshape(f32[3,3,2048]{2,1,0:T(4,128)} %param.14) | data formatting | bytes 147456 | tf_op jit(solution)/shard_map/reshape | solution.py:513
  3.2 0.0 copy-done.5
  3.2 0.0 copy-done.4
  3.2 0.0 copy-start.2
  3.2 0.0 copy-start.3
  3.2 0.1 fusion
  3.3 0.0 copy-start.1
  3.4 0.0 copy-start
  3.5 0.8 copy-done.2
  4.2 0.2 copy-done.3
  4.4 0.2 copy-done.1
  4.6 0.2 copy-done
  4.7 72.0 %shard_map.127 = (bf16[32,8192]{1,0:T(8,128)(2,1)S(1)}, bf16[32,8192]{1,0:T(8,128)(2,1)S(1)}, bf16[32,8192]{1,0:T(8,128)(2,1)S(1)}, bf16[32,8192]{1,0:T(8,128)(2...) custom-call(s32[130]{0:T(256)S(1)} %get-tuple-element.32.flags, f32[4,130]{1,0:T(4,128)S(1)} %add_convert_fusion.gates, ...), custom_call_target="tpu_custom_call" | custom-call | tf_op jit(solution)/shard_map/pallas_call | solution.py:525
  76.7 0.7 reshape.103
  77.4 0.8 copy.22
  78.2 0.8 copy.23
  79.0 0.8 copy.24
  79.8 0.8 copy.25
  80.5 0.7 copy.26
  (17 shorter events, 0.2 us)
Async XLA Ops:
  0.6 0.7 copy-start.6
  0.6 2.5 %copy-start.5 = (f32[16,2048]{1,0:T(8,128)S(1)}, f32[16,2048]{1,0:T(8,128)}, u32[]{:S(2)}) copy-start(f32[16,2048]{1,0:T(8,128)} %param.12) | copy-start | bytes 393220
  0.7 2.5 %copy-start.4 = (f32[16,2048]{1,0:T(8,128)S(1)}, f32[16,2048]{1,0:T(8,128)}, u32[]{:S(2)}) copy-start(f32[16,2048]{1,0:T(8,128)} %param.13) | copy-start | bytes 393220
  3.2 1.0 %copy-start.2 = (bf16[32,8192]{1,0:T(8,128)(2,1)S(1)}, bf16[32,8192]{1,0:T(8,128)(2,1)}, u32[]{:S(2)}) copy-start(bf16[32,8192]{1,0:T(8,128)(2,1)} %value_in.1) | copy-start | bytes 1572868
  3.2 1.2 %copy-start.3 = (bf16[32,8192]{1,0:T(8,128)(2,1)S(1)}, bf16[32,8192]{1,0:T(8,128)(2,1)}, u32[]{:S(2)}) copy-start(bf16[32,8192]{1,0:T(8,128)(2,1)} %cotangent.1) | copy-start | bytes 1572868
  3.3 1.3 %copy-start.1 = (bf16[32,8192]{1,0:T(8,128)(2,1)S(1)}, bf16[32,8192]{1,0:T(8,128)(2,1)}, u32[]{:S(2)}) copy-start(bf16[32,8192]{1,0:T(8,128)(2,1)} %key_in.1) | copy-start | bytes 1572868
  3.4 1.4 %copy-start = (bf16[32,8192]{1,0:T(8,128)(2,1)S(1)}, bf16[32,8192]{1,0:T(8,128)(2,1)}, u32[]{:S(2)}) copy-start(bf16[32,8192]{1,0:T(8,128)(2,1)} %query_in.1) | copy-start | bytes 1572868
where the time goes:
time: 81.4 us; the launch traced here: 81.2 us
  Pallas kernels  72 us (88%)
  local copies, waits for them, and re-layouts  7.6 us (9%)
  between operations  0.84 us (1%)
    pallas_call x1, Pallas kernels, shards(): pl.pallas_call(functools.partial(mixer, shape), out_shape=[jax.ShapeDtype...  72 us
    unnamed x22, local copies, waits for them, and re-layouts  5.86 us

commit v1 on v0

--- a/solution.py
+++ b/solution.py
@@ -10,7 +10,8 @@
 MESH = pl.DeviceIdType.MESH
 sub, lanes = 8, 128
 wide = sub * lanes
-step_rows = 4
+step_rows = 8
+most_vmem = 60 * 1024 * 1024
 
 
 def total_of(terms):
@@ -23,10 +24,11 @@
 
 def mixer(
     shape,
-    flags, gates, reach, query_in, key_in, value_in, cotangent, table, mixing, kappa, taps,
+    lengths, query_in, key_in, value_in, cotangent, decays, mixing_in, kappa_in, weights,
     output, d_query, d_key, d_value, d_resid, d_short,
     inbox, stage, rows, grads, feats, product, grad_pre, d_feat, outbox,
     state_send, state_recv, part, shares, summed, whole,
+    flags, gates, reach, flat, table, mixing, kappa, taps,
     in_send, in_recv, local_sem, tail_send, tail_recv, far_send, far_recv,
     head_send, head_recv, out_send, out_recv, share_send, share_recv, whole_send, whole_recv,
 ):
@@ -88,11 +90,71 @@
             sources[a].at[:, columns(chan, q)], inbox.at[a, q, chan], local_sem.at[0, q, a]
         )
 
-    for q in range(chunks):
+    def in_start(q):
         for a in range(4):
             for k in range(1, width):
                 in_copy(q, a, k).start()
             in_local(q, a).start()
+
+    in_start(0)
+
+    first = ctx * count
+    starts = [jnp.int32(0)]
+    for d in range(lengths.shape[0] - 1):
+        starts.append(starts[-1] + lengths[d])
+
+    def mark(x, carry):
+        position = first - rim + x
+        flags[x] = jnp.minimum(sum(jnp.where(position == s, 1, 0) for s in starts), 1)
+        return carry
+
+    lax.fori_loop(0, count + 2 * rim, mark, 0)
+
+    def open_gates(t, seen):
+        seen = seen + flags[t + rim]
+        gates[0, t] = jnp.where(seen == 0, 1.0, 0.0)
+        crossed = jnp.where(first + t < n * count, 0, 1)
+        for j in range(1, tap_count):
+            crossed = crossed + flags[t + rim - j + 1]
+            gates[j, t] = jnp.where(crossed == 0, 1.0, 0.0)
+        return seen
+
+    lax.fori_loop(0, count + rim, open_gates, jnp.int32(0))
+
+    def open_ends(x, seen):
+        t = count - 1 - x
+        gates[tap_count, t] = jnp.where(seen == 0, 1.0, 0.0)
+        return seen + flags[t + rim]
+
+    lax.fori_loop(0, count, open_ends, jnp.int32(0))
+
+    def open_reach(d, carry):
+        low = first - d * count
+        high = first + (d + 1) * count
+        early = sum(jnp.where((s >= low) & (s < first), 1, 0) for s in starts)
+        late = sum(jnp.where((s >= first + count) & (s < high), 1, 0) for s in starts)
+        reach[0, d] = jnp.where(early == 0, 1.0, 0.0)
+        reach[1, d] = jnp.where(late == 0, 1.0, 0.0)
+        return carry
+
+    lax.fori_loop(0, span, open_reach, 0)
+
+    tiles = chunks * sub
+    for x, origin in enumerate((decays, mixing_in, kappa_in)):
+        for j in range(tiles):
+            flat[x, pl.ds(j * modes, modes), :] = origin[:, pl.ds(j * lanes, lanes)]
+    for m in range(modes):
+        for q in range(chunks):
+            where = pl.ds(q * sub, sub)
+            picked = pl.ds(q * sub * modes + m, sub, stride=modes)
+            table[0, m, where, :] = flat[0, picked, :]
+            table[1, m, where, :] = jnp.zeros((sub, lanes), jnp.float32)
+            mixing[m, where, :] = flat[1, picked, :]
+            kappa[m, where, :] = flat[2, picked, :]
+    for i in range(3):
+        for j in range(tap_count):
+            for x in range(tiles):
+                taps[i * tap_count + j, pl.ds(x, 1), :] = weights[i, pl.ds(j, 1), pl.ds(x * lanes, lanes)]
 
     def tail_copy(q, i):
         return pltpu.make_async_remote_copy(
@@ -155,6 +217,8 @@
             for k in range(1, width):
                 in_arrival(q, a, k).wait_recv()
             in_local(q, a).wait()
+            if a == 3 and q + 1 < chunks:
+                in_start(q + 1)
 
         for a in range(4):
             def place(s, carry):
@@ -176,52 +240,53 @@
         lax.fori_loop(0, count // step_rows, lift, 0)
         for i in range(3):
             tail_copy(q, i).start()
-        for i in range(3):
-            tail_copy(q, i).wait_recv()
-
         decay = [table[0, m, mode_block(q), :] for m in range(modes)]
         tap = [[taps[i * tap_count + j, mode_block(q), :] for j in range(tap_count)] for i in range(3)]
+
+        def feature(i, t):
+            return tap[i][0] * rows[q, i, t + rim] + total_of(
+                [
+                    (gates[j, t] * tap[i][j]) * rows[q, i, t + rim - j]
+                    for j in range(1, tap_count)
+                ]
+            )
 
         def featurize(b, states):
             for u in range(step_rows):
                 t = b * step_rows + u
-                made = []
-                for i in range(3):
-                    made.append(
-                        tap[i][0] * rows[q, i, t + rim]
-                        + total_of(
-                            [
-                                (gates[j, t] * tap[i][j]) * rows[q, i, t + rim - j]
-                                for j in range(1, tap_count)
-                            ]
-                        )
-                    )
-                value = made[1] * made[2]
-                for i in range(3):
-                    feats[q, i, t] = made[i]
+                made = (feature(1, t), feature(2, t))
+                value = made[0] * made[1]
+                feats[q, 1, t] = made[0]
+                feats[q, 2, t] = made[1]
                 product[q, t] = value
-                grad_pre[q, t] = grads[q, t] * made[0]
                 masked = gates[tap_count, t] * value
                 states = tuple(decay[m] * states[m] + masked for m in range(modes))
             return states
 
         zeros = tuple(jnp.zeros((sub, lanes), jnp.float32) for _ in range(modes))
+        def back(b, states):
+            for u in range(step_rows):
+                t = count - 1 - b * step_rows - u
+                query = feature(0, t)
+                feats[q, 0, t] = query
+                value = grads[q, t] * query
+                grad_pre[q, t] = value
+                masked = gates[0, t] * value
+                states = tuple(decay[m] * states[m] + masked for m in range(modes))
+            return states
+
+        last = count // step_rows - 1
+        ends = lax.fori_loop(0, last, back, zeros)
+        for i in range(3):
+            tail_copy(q, i).wait_recv()
+        ends = lax.fori_loop(last, last + 1, back, ends)
+        for m in range(modes):
+            state_send[q, 1, m] = ends[m]
+        far_start(q, 1)
         ends = lax.fori_loop(0, count // step_rows, featurize, zeros)
         for m in range(modes):
             state_send[q, 0, m] = ends[m]
         far_start(q, 0)
-
-        def back(b, states):
-            for u in range(step_rows):
-                t = count - 1 - b * step_rows - u
-                masked = gates[0, t] * grad_pre[q, t]
-                states = tuple(decay[m] * states[m] + masked for m in range(modes))
-            return states
-
-        ends = lax.fori_loop(0, count // step_rows, back, zeros)
-        for m in range(modes):
-            state_send[q, 1, m] = ends[m]
-        far_start(q, 1)
 
     def entering(q, way):
         far_wait(q, way)
@@ -326,7 +391,7 @@
             states, sums = carry
             for u in range(step_rows):
                 t = count - 1 - b * step_rows - u
-                flag = flags[t + 1]
+                flag = flags[t + rim + 1]
                 grad_row = grad_pre[q, t]
                 states = tuple(
                     table[flag, m, mode_block(q), :] * states[m] + grad_row for m in range(modes)
@@ -352,7 +417,7 @@
             states, found, sums = carry
             for u in range(step_rows):
                 t = b * step_rows + u
-                flag = flags[t]
+                flag = flags[t + rim]
                 value = product[q, t]
                 grad_row = grad_pre[q, t]
                 states = tuple(
@@ -367,8 +432,9 @@
             return states, found, sums
 
         start = (carried, (zero,) * modes, (zero,) * tap_count)
-        _, found, sums = lax.fori_loop(0, count // step_rows, advance, start)
+        start = lax.fori_loop(0, 1, advance, start)
         head_copy(q, 0).start()
+        _, found, sums = lax.fori_loop(1, count // step_rows, advance, start)
         send_out(q, 0)
         for m in range(modes):
             put_part(q, m, kappa[m, mode_block(q), :] * found[m])
@@ -434,7 +500,7 @@
             x = modes + y
             value = whole[q, x // piece, x % piece]
             for j in range(sub):
-                d_short[pl.ds(y, 1), pl.ds((q * sub + j) * lanes, lanes)] = value[j : j + 1]
+                d_short[y // tap_count, pl.ds(y % tap_count, 1), pl.ds((q * sub + j) * lanes, lanes)] = value[j : j + 1]
 
     for q in range(chunks):
         first_pass(q)
@@ -470,6 +536,14 @@
         lax.fori_loop(1, n, drain, 0)
 
 
+def hand_over(*refs):
+    copies = [pltpu.make_async_copy(refs[x], refs[6 + x], refs[12].at[x]) for x in range(6)]
+    for copy in copies:
+        copy.start()
+    for copy in copies:
+        copy.wait()
+
+
 def shards(n, width, query_in, key_in, value_in, cotangent, residues, decay_rate, short_weight, doc_lengths):
     own_rows, channels = query_in.shape
     modes, local = residues.shape
@@ -479,45 +553,15 @@
     chunks = local // wide
     tiles = local // lanes
     span = max(n // 2, 1)
-    first_row = lax.axis_index("ctx") * count
-    order = jnp.arange(doc_lengths.shape[0], dtype=jnp.int32)
-    starts = jnp.sum(jnp.where(order[None, :] < order[:, None], doc_lengths[None, :], 0), axis=1)
-    positions = first_row - rim + jnp.arange(count + 2 * rim, dtype=jnp.int32)
-    hits = jnp.any(positions[:, None] == starts[None, :], axis=1)
-    after = positions[rim:]
-    gate_rows = []
-    behind = (after < n * count) & (after >= 0)
-    gate_rows_tail = []
-    keep = behind
-    for j in range(1, tap_count):
-        keep = keep & ~hits[rim - j + 1 : rim - j + 1 + count + rim]
-        gate_rows_tail.append(keep & (after >= j))
-    inside = (starts[None, :] >= first_row) & (starts[None, :] <= after[:, None])
-    gate_rows.append(~jnp.any(inside, axis=1))
-    gate_rows += gate_rows_tail
-    later = (starts[None, :] > after[:, None]) & (starts[None, :] < first_row + count)
-    gate_rows.append(~jnp.any(later, axis=1))
-    gates = jnp.stack(gate_rows).astype(jnp.float32)
-    flags = hits[rim:].astype(jnp.int32)
-    hop = jnp.arange(1, span + 1, dtype=jnp.int32)[:, None]
-    early = (starts[None, :] >= first_row - (hop - 1) * count) & (starts[None, :] < first_row)
-    late = (starts[None, :] >= first_row + count) & (starts[None, :] < first_row + hop * count)
-    reach = jnp.stack([~jnp.any(early, axis=1), ~jnp.any(late, axis=1)]).astype(jnp.float32)
-
     decays = jnp.exp(-decay_rate)
     kappa = jnp.sqrt(1.0 - jnp.exp(-2.0 * decay_rate))
     mixing = residues * kappa
-    table = jnp.stack([decays, jnp.zeros_like(decays)]).reshape(2, modes, tiles, lanes)
-    mixing = mixing.reshape(modes, tiles, lanes)
-    kappa = kappa.reshape(modes, tiles, lanes)
-    taps = short_weight.reshape(3 * tap_count, tiles, lanes)
-
     pieces = modes + 3 * tap_count
     piece = -(-pieces // n)
     pitch = count + 8
     f32, bf16 = jnp.float32, jnp.bfloat16
     dma = pltpu.SemaphoreType.DMA
-    anywhere = pl.BlockSpec(memory_space=pl.ANY)
+    anywhere = pl.BlockSpec(memory_space=pltpu.HBM)
     vmem = pl.BlockSpec(memory_space=pltpu.VMEM)
     smem = pl.BlockSpec(memory_space=pltpu.SMEM)
     shape = (n, width, span, count, modes, tap_count, piece, chunks)
@@ -527,9 +571,9 @@
         out_shape=[jax.ShapeDtypeStruct((own_rows, channels), bf16)] * 4
         + [
             jax.ShapeDtypeStruct((modes, local), f32),
-            jax.ShapeDtypeStruct((3 * tap_count, local), f32),
+            jax.ShapeDtypeStruct(short_weight.shape, f32),
         ],
-        in_specs=[smem] * 3 + [anywhere] * 4 + [vmem] * 4,
+        in_specs=[smem] + [anywhere] * 4 + [vmem] * 4,
         out_specs=[anywhere] * 4 + [vmem] * 2,
         scratch_shapes=[
             pltpu.VMEM((4, chunks, width, own_rows, wide), bf16),
@@ -547,6 +591,14 @@
             pltpu.VMEM((chunks, n, piece) + token, f32),
             pltpu.VMEM((chunks, piece) + token, f32),
             pltpu.VMEM((chunks, n, piece) + token, f32),
+            pltpu.SMEM((count + 2 * rim,), jnp.int32),
+            pltpu.SMEM((tap_count + 1, count + rim), f32),
+            pltpu.SMEM((2, span), f32),
+            pltpu.VMEM((3, tiles * modes, lanes), f32),
+            pltpu.VMEM((2, modes, tiles, lanes), f32),
+            pltpu.VMEM((modes, tiles, lanes), f32),
+            pltpu.VMEM((modes, tiles, lanes), f32),
+            pltpu.VMEM((3 * tap_count, tiles, lanes), f32),
             dma((chunks, 4, width)),
             dma((chunks, 4, width)),
             dma((2, chunks, 4)),
@@ -564,10 +616,17 @@
             dma((chunks, n)),
         ],
         compiler_params=pltpu.CompilerParams(
-            collective_id=0, has_side_effects=True, vmem_limit_bytes=48 * 1024 * 1024
+            collective_id=0, has_side_effects=True, vmem_limit_bytes=most_vmem
         ),
-    )(flags, gates, reach, query_in, key_in, value_in, cotangent, table, mixing, kappa, taps)
-    return (*results[:5], results[5].reshape(short_weight.shape))
+    )(doc_lengths, query_in, key_in, value_in, cotangent, decays, mixing, kappa, short_weight)
+    return pl.pallas_call(
+        hand_over,
+        out_shape=[jax.ShapeDtypeStruct(r.shape, r.dtype) for r in results],
+        in_specs=[vmem] * 6,
+        out_specs=[anywhere] * 6,
+        scratch_shapes=[dma((6,))],
+        compiler_params=pltpu.CompilerParams(vmem_limit_bytes=most_vmem),
+    )(*results)
 
 
 def solution(mesh):

time: 81.4 us -> 75.8 us (0.931)
  local copies, waits for them, and re-layouts: 7.6 us -> 0 us
  Pallas kernels: 72 us -> 73.2 us
  other arithmetic: 0.81 us -> 1.77 us
    unnamed x22 -> x0, local copies, waits for them, and re-layouts: 5.86 us -> none
    pallas_call x0 -> x1, Pallas kernels: none -> 2.99 us  [shards(): pl.pallas_call(hand_over, out_shape=[jax.ShapeDtypeStruct(r.shape, r.dtyp...]
    sqrt x0 -> x1, other arithmetic: none -> 1.77 us  [shards(): kappa = jnp.sqrt(1.0 - jnp.exp(-2.0 * decay_rate))]
    pallas_call x1, Pallas kernels: 72 us -> 70.2 us  [shards(): pl.pallas_call(functools.partial(mixer, shape), out_shape=[jax.ShapeDtype...]
    reshape x2 -> x0, local copies, waits for them, and re-layouts: 1.62 us -> none  [the longest x1 0.95 us: shards(): taps = short_weight.reshape(3 * tap_count, tiles, lanes)]
where the time goes in v1:
time: 75.8 us; the launch traced here: 75.6 us
  Pallas kernels  73.2 us (97%)
  other arithmetic  1.77 us (2%)
    pallas_call x1, Pallas kernels, shards(): pl.pallas_call(functools.partial(mixer, shape), out_shape=[jax.ShapeDtype...  70.2 us
    pallas_call x1, Pallas kernels, shards(): pl.pallas_call(hand_over, out_shape=[jax.ShapeDtypeStruct(r.shape, r.dtyp...  2.99 us
    sqrt x1, other arithmetic, shards(): kappa = jnp.sqrt(1.0 - jnp.exp(-2.0 * decay_rate))  1.77 us

profile of v1, /device:TPU:13, one launch (start us, length us, event | category | flops | bytes accessed | tf_op | source)
XLA Modules:
  0.0 75.6 jit_solution(464787491345333464)
XLA Ops:
  0.6 1.8 %subtract_sqrt_fusion = (f32[16,2048]{1,0:T(8,128)}, f32[16,2048]{1,0:T(8,128)}, f32[16,2048]{1,0:T(8,128)}) fusion(f32[16,2048]{1,0:T(8,128)} %param.13, f32[16,2048]{1,0:T(8,128)} %param.12), kind=kLoop, calls=%fused_computation | loop fusion | flops 131072 | bytes 655360 | tf_op jit(solution)/shard_map/sqrt | solution.py:557
  2.4 70.2 %shard_map.127 = (bf16[32,8192]{1,0:T(8,128)(2,1)}, bf16[32,8192]{1,0:T(8,128)(2,1)}, bf16[32,8192]{1,0:T(8,128)(2,1)}, bf16[32,8192]{1,0:T(8,128)(2,1)}, f32[16,2048]{1,0:T(8,128)}, /*index=5*/f32[3,3,2048]{2,1,0:T(4,128)}) custom-call(s32[8]{0:T(128)} %lengths.1, bf16[32,8192]{1,0:T(8,128)(2,1)} %query_in.1, bf16[32,8192]{1,0:T(8,128)(2,1)} %key_in.1, ...), custom_call_target="tpu_custom_call" | custom-call | tf_op jit(solution)/shard_map/pallas_call | solution.py:569
  72.6 3.0 %shard_map.128 = (bf16[32,8192]{1,0:T(8,128)(2,1)}, bf16[32,8192]{1,0:T(8,128)(2,1)}, bf16[32,8192]{1,0:T(8,128)(2,1)}, bf16[32,8192]{1,0:T(8,128)(2,1)}, f32[16,2048]{1,0:T(8,128)}, /*index=5*/f32[3,3,2048]{2,1,0:T(4,128)}) custom-call(bf16[32,8192]{1,0:T(8,128)(2,1)} %get-tuple-element.12.refs_0_, bf16[32,8192]{1,0:T(8,128)(2,1)} %get-tuple-element.13.refs_1_, ...), custom_call_target="tpu_custom_call" | custom-call | tf_op jit(solution)/shard_map/pallas_call | solution.py:622

commit v2 on v1

--- a/solution.py
+++ b/solution.py
@@ -92,7 +92,7 @@
 
     def in_start(q):
         for a in range(4):
-            for k in range(1, width):
+            for k in sorted(range(1, width), key=lambda k: abs(2 * k - width)):
                 in_copy(q, a, k).start()
             in_local(q, a).start()
 
@@ -374,7 +374,7 @@
             return carry
 
         lax.fori_loop(0, width, pack, 0)
-        for k in range(1, width):
+        for k in sorted(range(1, width), key=lambda k: abs(2 * k - width)):
             out_copy(q, a, k).start()
         out_local(q, a).start()
 

time: 75.8 us -> 74.9 us (0.988)
  Pallas kernels: 73.2 us -> 72.3 us
    pallas_call x1, Pallas kernels: 70.2 us -> 69.3 us  [shards(): pl.pallas_call(functools.partial(mixer, shape), out_shape=[jax.ShapeDtype...]
where the time goes in v2:
time: 74.9 us; the launch traced here: 74.7 us
  Pallas kernels  72.3 us (97%)
  other arithmetic  1.77 us (2%)
    pallas_call x1, Pallas kernels, shards(): pl.pallas_call(functools.partial(mixer, shape), out_shape=[jax.ShapeDtype...  69.3 us
    pallas_call x1, Pallas kernels, shards(): pl.pallas_call(hand_over, out_shape=[jax.ShapeDtypeStruct(r.shape, r.dtyp...  2.99 us
    sqrt x1, other arithmetic, shards(): kappa = jnp.sqrt(1.0 - jnp.exp(-2.0 * decay_rate))  1.77 us

profile of v2, /device:TPU:13, one launch (start us, length us, event | category | flops | bytes accessed | tf_op | source)
XLA Modules:
  0.0 74.7 jit_solution(3113790892764903270)
XLA Ops:
  0.6 1.8 %subtract_sqrt_fusion = (f32[16,2048]{1,0:T(8,128)}, f32[16,2048]{1,0:T(8,128)}, f32[16,2048]{1,0:T(8,128)}) fusion(f32[16,2048]{1,0:T(8,128)} %param.13, f32[16,2048]{1,0:T(8,128)} %param.12), kind=kLoop, calls=%fused_computation | loop fusion | flops 131072 | bytes 655360 | tf_op jit(solution)/shard_map/sqrt | solution.py:557
  2.4 69.3 %shard_map.127 = (bf16[32,8192]{1,0:T(8,128)(2,1)}, bf16[32,8192]{1,0:T(8,128)(2,1)}, bf16[32,8192]{1,0:T(8,128)(2,1)}, bf16[32,8192]{1,0:T(8,128)(2,1)}, f32[16,2048]{1,0:T(8,128)}, /*index=5*/f32[3,3,2048]{2,1,0:T(4,128)}) custom-call(s32[8]{0:T(128)} %lengths.1, bf16[32,8192]{1,0:T(8,128)(2,1)} %query_in.1, bf16[32,8192]{1,0:T(8,128)(2,1)} %key_in.1, ...), custom_call_target="tpu_custom_call" | custom-call | tf_op jit(solution)/shard_map/pallas_call | solution.py:569
  71.7 3.0 %shard_map.128 = (bf16[32,8192]{1,0:T(8,128)(2,1)}, bf16[32,8192]{1,0:T(8,128)(2,1)}, bf16[32,8192]{1,0:T(8,128)(2,1)}, bf16[32,8192]{1,0:T(8,128)(2,1)}, f32[16,2048]{1,0:T(8,128)}, /*index=5*/f32[3,3,2048]{2,1,0:T(4,128)}) custom-call(bf16[32,8192]{1,0:T(8,128)(2,1)} %get-tuple-element.12.refs_0_, bf16[32,8192]{1,0:T(8,128)(2,1)} %get-tuple-element.13.refs_1_, ...), custom_call_target="tpu_custom_call" | custom-call | tf_op jit(solution)/shard_map/pallas_call | solution.py:622
